TPU v7x, 256 devices: a whole 4x4x8 slice. The times are simulated.
256 devices in a mesh: gx: 8 (over z_hi, core), gy: 32 (over z_lo, y, x).
Axes of the slice: x: 4, y: 4, z: 8 (z_hi: 4, z_lo: 2; z = z_hi * 2 + z_lo), core: 2. Of those that a mesh axis runs over, the one named last changes fastest.
Arguments:
- inputs: bfloat16 [1024, 4096], P('gy', 'gx'), may hold values from -6 to 6
- cotangent: bfloat16 [1024, 4096], P('gy', 'gx'), may hold values from -6 to 6
- gate_weight: bfloat16 [4096, 16384], P('gx', 'gy'), may hold values from -0.09375 to 0.09375
- up_weight: bfloat16 [4096, 16384], P('gx', 'gy'), may hold values from -0.09375 to 0.09375
- down_weight: bfloat16 [16384, 4096], P('gy', 'gx'), may hold values from -0.046875 to 0.046875
Outputs:
- input_grad: bfloat16 [1024, 4096], P('gy', 'gx')
- gate_grad: bfloat16 [4096, 16384], P('gx', 'gy')
- up_grad: bfloat16 [4096, 16384], P('gx', 'gy')
- down_grad: bfloat16 [16384, 4096], P('gy', 'gx')
All inputs are finite; a program needn't handle non-finite values.
Results may differ from a plain program's by a relative error of at most 0.0049.
Values may be sent and summed in bfloat16 or wider, within the bound.
A program may use at most 64 MiB of HBM per device.

v0:
```python
import jax
import jax.numpy as jnp
from jax import lax
from jax.sharding import PartitionSpec as P


def local_hidden(sums, width):
    gate = sums[:, :width]
    up_sum = sums[:, width : 2 * width]
    dhidden = sums[:, 2 * width :]
    coeff = jnp.float32(0.7978845608028654)
    inner = coeff * (gate + 0.044715 * gate * gate * gate)
    tanh_val = jnp.tanh(inner)
    act = 0.5 * gate * (1.0 + tanh_val)
    slope = 0.5 * (1.0 + tanh_val) + 0.5 * gate * (1.0 - tanh_val * tanh_val) * coeff * (
        1.0 + 3.0 * 0.044715 * gate * gate
    )
    hidden = (act * up_sum).astype(jnp.bfloat16)
    dgate = (dhidden * up_sum * slope).astype(jnp.bfloat16)
    dup = (dhidden * act).astype(jnp.bfloat16)
    return (hidden, jnp.concatenate([dgate, dup], axis=1))


def local(inputs, cotangent, gate_weight, up_weight, down_weight):
    gathered, cot_rows = (
        lax.all_gather(inputs, "gy", axis=0, tiled=True),
        lax.all_gather(cotangent, "gy", axis=0, tiled=True),
    )
    width = gate_weight.shape[1]
    both_weight = jnp.concatenate([gate_weight, up_weight], axis=1)
    first = jnp.dot(gathered, both_weight, preferred_element_type=jnp.float32)
    second = lax.dot_general(
        cot_rows, down_weight, (((1,), (1,)), ((), ())), preferred_element_type=jnp.float32
    )
    sums = lax.psum_scatter(
        jnp.concatenate([first, second], axis=1), "gx", scatter_dimension=0, tiled=True
    )
    own_hidden, own_grads = local_hidden(sums, width)
    hidden, grads_both = (
        lax.all_gather(own_hidden, "gx", axis=0, tiled=True),
        lax.all_gather(own_grads, "gx", axis=0, tiled=True),
    )
    down_grad = lax.dot_general(
        hidden, cot_rows, (((0,), (0,)), ((), ())), preferred_element_type=jnp.float32
    ).astype(jnp.bfloat16)
    both_grad = lax.dot_general(
        gathered, grads_both, (((0,), (0,)), ((), ())), preferred_element_type=jnp.float32
    ).astype(jnp.bfloat16)
    gate_grad = both_grad[:, :width]
    up_grad = both_grad[:, width:]
    input_grad = lax.psum_scatter(
        lax.dot_general(
            grads_both, both_weight, (((1,), (1,)), ((), ())), preferred_element_type=jnp.float32
        ),
        "gy",
        scatter_dimension=0,
        tiled=True,
    ).astype(jnp.bfloat16)
    return (input_grad, gate_grad, up_grad, down_grad)


def solution(mesh):
    in_specs = (P("gy", "gx"), P("gy", "gx"), P("gx", "gy"), P("gx", "gy"), P("gy", "gx"))
    out_specs = (P("gy", "gx"), P("gx", "gy"), P("gx", "gy"), P("gy", "gx"))
    return jax.shard_map(local, mesh=mesh, in_specs=in_specs, out_specs=out_specs, check_vma=False)
```

profile of v0, /device:TPU:2, one launch (start us, length us, event | category | flops | bytes accessed | tf_op | source)
XLA Modules:
  0.0 653.9 jit_solution(5136610148849222048)
XLA Ops:
  7.2 0.7 all-gather.7.cloned.1.call-update
  8.0 0.7 all-gather.5.cloned.1.call-update
  8.7 1.9 constant_dynamic-update-slice_fusion.1
  10.6 1.9 constant_dynamic-update-slice_fusion
  12.6 153.5 %all-gather.7.cloned.1.call-done = bf16[1024,512]{1,0:T(8,128)(2,1)} async-done(((bf16[32,512]{1,0:T(8,128)(2,1)}), bf16[1024,512]{1,0:T(8,128)(2,1)}) %all-gather.7.cloned.1.call-update) | async-done | bytes 1048592 | tf_op jit(solution)/shard_map/all_gather | solution.py:27
  166.0 2.0 fusion.9
  168.0 153.7 %all-gather.5.cloned.1.call-done = bf16[1024,512]{1,0:T(8,128)(2,1)} async-done(((bf16[32,512]{1,0:T(8,128)(2,1)}), bf16[1024,512]{1,0:T(8,128)(2,1)}) %all-gather.5.cloned.1.call-update) | async-done | bytes 1048592 | tf_op jit(solution)/shard_map/all_gather | solution.py:26
  321.7 2.8 convolution_bitcast_fusion
  324.5 3.5 pad_maximum_fusion
  328.0 0.0 all-gather.9.cloned.1.call-start
  328.1 81.2 %reduce-scatter.3.cloned.1.call-done = f32[128,1536]{0,1:T(8,128)} async-done(((f32[1024,1536]{0,1:T(8,128)}), f32[128,1536]{0,1:T(8,128)}) %reduce-scatter.3.cloned.1.call-update) | async-done | bytes 786448 | tf_op jit(solution)/shard_map/reduce_scatter | solution.py:35
  409.2 2.0 multiply_convert_fusion
  411.2 0.7 pad_maximum_fusion.1
  412.0 0.5 all-gather.11.cloned.1.call-update
  412.6 39.7 %all-gather.9.cloned.1.call-done = bf16[1024,1024]{0,1:T(8,128)(2,1)} async-done(((bf16[128,1024]{0,1:T(8,128)(2,1)}), bf16[1024,1024]{0,1:T(8,128)(2,1)}) %all-gather.9.cloned.1.call-update) | async-done | bytes 2097168 | tf_op jit(solution)/shard_map/all_gather | solution.py:41
  452.4 4.5 fusion.10
  456.9 26.5 %all-gather.11.cloned.1.call-done = bf16[1024,512]{0,1:T(8,128)(2,1)} async-done(((bf16[128,512]{0,1:T(8,128)(2,1)}), bf16[1024,512]{0,1:T(8,128)(2,1)}) %all-gather.11.cloned.1.call-update) | async-done | bytes 1048592 | tf_op jit(solution)/shard_map/all_gather | solution.py:40
  483.4 2.9 convolution_convert_fusion.1
  486.3 1.2 fusion
  487.5 0.1 fusion.8
  487.6 1.0 copy.10
  488.6 1.0 copy.9
  489.6 156.0 %reduce-scatter.5.cloned.1.call-done = f32[32,512]{1,0:T(8,128)} async-done(((f32[1024,512]{1,0:T(8,128)}), f32[32,512]{1,0:T(8,128)}) %reduce-scatter.5.cloned.1.call-update) | async-done | bytes 65552 | tf_op jit(solution)/shard_map/reduce_scatter | solution.py:51
  645.6 1.5 convert_element_type.23
  (16 shorter events, 0.3 us)
Async XLA Ops:
  7.2 158.9 %copy-start = (bf16[512,512]{1,0:T(8,128)(2,1)S(1)}, bf16[512,512]{1,0:T(8,128)(2,1)}, u32[]{:S(2)}) copy-start(bf16[512,512]{1,0:T(8,128)(2,1)} %param.9) | copy-start | bytes 1572868
  7.2 158.9 %all-gather.7.cloned.1.call-start = ((), (), s32[]{:S(2)}) async-start(), calls=%async_computation.3 | async-start | bytes 1081344 | tf_op jit(solution)/shard_map/all_gather | solution.py:27
  7.9 313.8 %all-gather.5.cloned.1.call-start = ((), (), s32[]{:S(2)}) async-start(), calls=%async_computation.2 | async-start | bytes 1081344 | tf_op jit(solution)/shard_map/all_gather | solution.py:26
  8.7 400.6 %reduce-scatter.3.cloned.1.call-start = ((), (), s32[]{:S(2)}) async-start(), calls=%async_computation.4 | async-start | bytes 7077888 | tf_op jit(solution)/shard_map/reduce_scatter | solution.py:35
  328.0 124.4 %all-gather.9.cloned.1.call-start = ((), (), s32[]{:S(2)}) async-start(), calls=%async_computation.5 | async-start | bytes 2359296 | tf_op jit(solution)/shard_map/all_gather | solution.py:41
  412.0 71.4 %all-gather.11.cloned.1.call-start = ((), (), s32[]{:S(2)}) async-start(), calls=%async_computation.7 | async-start | bytes 1179648 | tf_op jit(solution)/shard_map/all_gather | solution.py:40
  412.6 233.0 %reduce-scatter.5.cloned.1.call-start = ((), (), s32[]{:S(2)}) async-start(), calls=%async_computation.6 | async-start | bytes 2162688 | tf_op jit(solution)/shard_map/reduce_scatter | solution.py:51
  456.8 26.6 %copy-start.1 = (bf16[1024,512]{1,0:T(8,128)(2,1)S(1)}, bf16[1024,512]{1,0:T(8,128)(2,1)}, u32[]{:S(2)}) copy-start(bf16[1024,512]{1,0:T(8,128)(2,1)} %all-gather.7.cloned.1.call-done) | copy-start | bytes 3145732
  456.9 29.4 %copy-start.3 = (bf16[1024,512]{1,0:T(8,128)(2,1)S(1)}, bf16[1024,512]{1,0:T(8,128)(2,1)}, u32[]{:S(2)}) copy-start(bf16[1024,512]{1,0:T(8,128)(2,1)} %all-gather.5.cloned.1.call-done) | copy-start | bytes 3145732
  483.4 2.9 copy-start.2
Sparse Core Ops, SparseCore 0:
  9.8 156.1 all-gather.6
  167.8 153.7 all-gather.4
  328.1 81.0 reduce-scatter.2
  412.1 40.2 all-gather.8
  454.6 28.7 all-gather.10
  485.7 159.7 reduce-scatter.4
where the time goes:
time: 658 us; the launch traced here: 654 us
  waiting for transfers between devices  613 us (93%)
  between operations  14.2 us (2%)
  matrix products  13.4 us (2%)
  other arithmetic  7.63 us (1%)
    reduce_scatter x1, waiting for transfers between devices, local(): lax.psum_scatter(lax.dot_general(grads_both, both_weight, (((1,), (1,)),...  156 us
    all_gather x1, waiting for transfers between devices, local(): lax.all_gather(inputs, 'gy', axis=0, tiled=True)  154 us
    all_gather x1, waiting for transfers between devices, local(): lax.all_gather(cotangent, 'gy', axis=0, tiled=True)  153 us
    reduce_scatter x1, waiting for transfers between devices, local(): lax.psum_scatter(jnp.concatenate([first, second], axis=1), 'gx', scatter_...  81.2 us
    all_gather x1, waiting for transfers between devices, local(): lax.all_gather(own_grads, 'gx', axis=0, tiled=True)  39.7 us
    all_gather x1, waiting for transfers between devices, local(): lax.all_gather(own_hidden, 'gx', axis=0, tiled=True)  26.5 us
  transfers between devices with their start and end apart: 6, of which 6 were waited for; matrix products, arithmetic and copies ran while one was open for 3% of the time, Pallas kernels for 0%

commit v1 on v0

v1 whole, which is shorter than its diff:
```python
import functools

import jax
import jax.numpy as jnp
from jax import lax
from jax.experimental import pallas as pl
from jax.experimental.pallas import tpu as pltpu
from jax.sharding import PartitionSpec as P

MESH = pl.DeviceIdType.MESH
F32, BF16 = jnp.float32, jnp.bfloat16
D = 512
F = 512
FH = F // 2
OWN = 32
TC = 2 * OWN
N = 16
Q = TC // 4
W3 = 3 * FH
WH = W3 // 2
GROUP = 4
OFF_B, OFF_C, OFF_D, OFF_E, OFF_F, OFF_G = 2, 4, 6, 8, 9, 11


def dot(a, b, dims):
    return lax.dot_general(a, b, (dims, ((), ())), preferred_element_type=F32)


def gelu_parts(gate, up_sum, dhidden):
    coeff = jnp.float32(0.7978845608028654)
    inner = coeff * (gate + 0.044715 * gate * gate * gate)
    tanh_val = jnp.tanh(inner)
    act = 0.5 * gate * (1.0 + tanh_val)
    slope = 0.5 * (1.0 + tanh_val) + 0.5 * gate * (1.0 - tanh_val * tanh_val) * coeff * (
        1.0 + 3.0 * 0.044715 * gate * gate
    )
    return act * up_sum, dhidden * up_sum * slope, dhidden * act


def kernel(
    x_in, cot_in, wg_in, wu_in, wd_in,
    ig_out, gg_out, ug_out, dg_out,
    tok, wgu, wd, part, s1, r1, s2, r2, hid, igs, igr, acc, igz, gu, dn, gu_o, dn_o, ig_o,
    loc, zl_s, zl_r, wx_s, wx_r, sx_s, sx_r, xs, xr, r1s, r1r, r2s, r2r, a1s, a1r, a2s, a2r, hs, hr, gs, gr, gz_s, gz_r, outs,
):
    gx, gy = lax.axis_index("gx"), lax.axis_index("gy")
    zh, core = gx // 2, gx % 2
    zl, y, x = gy // 16, (gy // 4) % 4, gy % 4

    def ring(step):
        return (((zh + step + 4) % 4) * 2 + core, gy)

    def plane(dy, dx):
        return (gx, zl * 16 + ((y + dy + 4) % 4) * 4 + (x + dx + 4) % 4)

    sibling = (zh * 2 + 1 - core, gy)
    partner = (gx, (1 - zl) * 16 + y * 4 + x)

    def remote(src, dst, send, recv, device):
        return pltpu.make_async_remote_copy(
            src_ref=src, dst_ref=dst, send_sem=send, recv_sem=recv, device_id=device, device_id_type=MESH
        )

    barrier = pltpu.get_barrier_semaphore()
    for device in [ring(1), ring(-1), sibling, partner] + [plane(r // 4, r % 4) for r in range(1, N)]:
        pl.semaphore_signal(barrier, inc=1, device_id=device, device_id_type=MESH)

    mine = pl.ds(pl.multiple_of(core * FH, FH), FH)
    other = pl.ds(pl.multiple_of((1 - core) * FH, FH), FH)
    loads = [
        (x_in, tok.at[0, 0, pl.ds(0, OWN)]),
        (cot_in, tok.at[0, 1, pl.ds(0, OWN)]),
        (wg_in.at[:, other], wgu.at[1, :, pl.ds(0, FH)]),
        (wu_in.at[:, other], wgu.at[1, :, pl.ds(FH, FH)]),
        (wd_in.at[other], wd.at[1]),
        (wg_in.at[:, mine], wgu.at[0, :, pl.ds(0, FH)]),
        (wu_in.at[:, mine], wgu.at[0, :, pl.ds(FH, FH)]),
        (wd_in.at[mine], wd.at[0]),
    ]
    loads = [pltpu.make_async_copy(src, dst, loc.at[i]) for i, (src, dst) in enumerate(loads)]
    for load in loads:
        load.start()
    gu[...] = jnp.zeros_like(gu)
    dn[...] = jnp.zeros_like(dn)
    for load in loads:
        load.wait()
    pl.semaphore_wait(barrier, 4 + N - 1)

    first, second = pl.ds(0, OWN), pl.ds(OWN, OWN)
    to_partner = remote(tok.at[0, :, first], tok.at[0, :, second], zl_s, zl_r, partner)
    to_partner.start()
    own_sib = remote(tok.at[0, :, first], tok.at[1, :, first], sx_s.at[N], sx_r.at[N], sibling)
    own_sib.start()
    w_sib = [
        remote(wgu.at[1], wgu.at[2], wx_s.at[0], wx_r.at[0], sibling),
        remote(wd.at[1], wd.at[2], wx_s.at[1], wx_r.at[1], sibling),
    ]
    for copy in w_sib:
        copy.start()
    to_partner.wait_recv()
    pair_sib = remote(tok.at[0, :, second], tok.at[1, :, second], sx_s.at[0], sx_r.at[0], sibling)
    pair_sib.start()

    def rows(k):
        return pl.ds(pl.multiple_of(k * TC, TC), TC)

    def spread(k):
        return remote(tok.at[0, :, pl.ds(0, TC)], tok.at[0, :, rows(k)], xs.at[k], xr.at[k], plane(k // 4, k % 4))

    def start_spread(k, carry):
        spread(k).start()
        return carry

    lax.fori_loop(1, N, start_spread, 0)

    def forward(k):
        return remote(tok.at[0, :, rows(k)], tok.at[1, :, rows(k)], sx_s.at[k], sx_r.at[k], sibling)

    lo, hi = pl.ds(0, WH), pl.ds(WH, WH)

    def quarter(k, step):
        return pl.ds(pl.multiple_of(k * TC + ((zh + step + 4) % 4) * Q, Q), Q)

    def reduce1(k):
        return (
            remote(s1.at[k, :, lo], r1.at[k, :, lo], r1s.at[k, 0], r1r.at[k, 0], ring(1)),
            remote(s1.at[k, :, hi], r1.at[k, :, hi], r1s.at[k, 1], r1r.at[k, 1], ring(-1)),
        )

    def reduce2(k):
        return (
            remote(s2.at[k, 0], r2.at[k, 0], r2s.at[k, 0], r2r.at[k, 0], ring(1)),
            remote(s2.at[k, 1], r2.at[k, 1], r2s.at[k, 1], r2r.at[k, 1], ring(-1)),
        )

    def gather1(k, step):
        part_of = hid.at[0, quarter(k, step)]
        return (
            remote(part_of, part_of, a1s.at[k, 0], a1r.at[k, 0], ring(1)),
            remote(part_of, part_of, a1s.at[k, 1], a1r.at[k, 1], ring(-1)),
        )

    def gather2(k, up_step, down_step):
        up_half, down_half = hid.at[0, quarter(k, up_step), lo], hid.at[0, quarter(k, down_step), hi]
        return (
            remote(up_half, up_half, a2s.at[k, 0], a2r.at[k, 0], ring(1)),
            remote(down_half, down_half, a2s.at[k, 1], a2r.at[k, 1], ring(-1)),
        )

    def across(k):
        return remote(hid.at[0, rows(k)], hid.at[1, rows(k)], hs.at[k], hr.at[k], sibling)

    def give(k):
        return remote(igs.at[k], igr.at[k], gs.at[k], gr.at[k], plane(-(k // 4), -(k % 4)))

    def stage_x(k):
        @pl.when(k > 0)
        def _():
            spread(k).wait_recv()
            forward(k).start()

    def stage_a(k):
        @pl.when(k == 0)
        def _():
            own_sib.wait_recv()
            pair_sib.wait_recv()
            for copy in w_sib:
                copy.wait_recv()

        @pl.when(k > 0)
        def _():
            forward(k).wait_recv()

        here = rows(k)
        both = ((1,), (0,))
        back = ((1,), (1,))
        part[here, : 2 * FH] = dot(tok[0, 0, here], wgu[0], both) + dot(tok[1, 0, here], wgu[2], both)
        part[here, 2 * FH :] = dot(tok[0, 1, here], wd[0], back) + dot(tok[1, 1, here], wd[2], back)
        s1[k] = part[quarter(k, 2)].astype(BF16)
        for copy in reduce1(k):
            copy.start()

    def stage_b(k):
        for copy in reduce1(k):
            copy.wait_recv()
        ahead, behind = part[quarter(k, 1)], part[quarter(k, -1)]
        got = r1[k].astype(F32)
        s2[k, 0, :, :WH] = (ahead[:, :WH] + got[:, :WH]).astype(BF16)
        s2[k, 0, :, WH:] = ahead[:, WH:].astype(BF16)
        s2[k, 1, :, :WH] = behind[:, :WH].astype(BF16)
        s2[k, 1, :, WH:] = (behind[:, WH:] + got[:, WH:]).astype(BF16)
        for copy in reduce2(k):
            copy.start()

    def stage_c(k):
        for copy in reduce2(k):
            copy.wait_recv()
        sums = part[quarter(k, 0)] + r2[k, 0].astype(F32) + r2[k, 1].astype(F32)
        hidden, dgate, dup = gelu_parts(sums[:, :FH], sums[:, FH : 2 * FH], sums[:, 2 * FH :])
        own = quarter(k, 0)
        hid[0, own, :FH] = hidden.astype(BF16)
        hid[0, own, FH : 2 * FH] = dgate.astype(BF16)
        hid[0, own, 2 * FH :] = dup.astype(BF16)
        for copy in gather1(k, 0):
            copy.start()

    def stage_d(k):
        gather1(k, -1)[0].wait_recv()
        gather1(k, 1)[1].wait_recv()
        for copy in gather2(k, -1, 1):
            copy.start()

    def stage_e(k):
        for copy in gather2(k, 2, 2):
            copy.wait_recv()
        across(k).start()

    def stage_f(k):
        across(k).wait_recv()
        here = rows(k)
        back = ((1,), (1,))
        share = dot(hid[0, here, FH:], wgu[0], back) + dot(hid[1, here, FH:], wgu[1], back)

        @pl.when(k == 0)
        def _():
            acc[...] = share

        @pl.when(k > 0)
        def _():
            igs[k] = share.astype(BF16)
            give(k).start()

        @pl.when(k % GROUP == GROUP - 1)
        def _():
            block = pl.ds(pl.multiple_of((k // GROUP) * GROUP * TC, GROUP * TC), GROUP * TC)
            over = ((0,), (0,))
            for h in range(2):
                gu[h] += dot(tok[0, 0, block], hid[h, block, FH:], over)
                dn[h] += dot(hid[h, block, :FH], tok[0, 1, block], over)

        @pl.when(k == N - 1)
        def _():
            gu_o[...] = gu[...].astype(BF16)
            dn_o[...] = dn[...].astype(BF16)
            for copy in results():
                copy.start()

    def results():
        copies = []
        for h, cols in enumerate((mine, other)):
            copies += [
                (gu_o.at[h, :, pl.ds(0, FH)], gg_out.at[:, cols]),
                (gu_o.at[h, :, pl.ds(FH, FH)], ug_out.at[:, cols]),
                (dn_o.at[h], dg_out.at[cols]),
            ]
        return [pltpu.make_async_copy(src, dst, outs.at[i]) for i, (src, dst) in enumerate(copies)]

    def stage_g(k):
        @pl.when(k > 0)
        def _():
            give(k).wait_recv()
            acc[...] += igr[k].astype(F32)
            give(k).wait_send()
            spread(k).wait_send()
            forward(k).wait_send()

        for copy in reduce1(k) + reduce2(k) + gather1(k, 0) + gather2(k, -1, 1) + (across(k),):
            copy.wait_send()

    def step(s, carry):
        def at(offset, stage):
            k = s - offset

            @pl.when(jnp.logical_and(k >= 0, k < N))
            def _():
                stage(k)

        at(0, stage_x)
        at(OFF_B, stage_b)
        at(OFF_C, stage_c)
        at(OFF_D, stage_d)
        at(OFF_E, stage_e)
        at(0, stage_a)
        at(OFF_F, stage_f)
        at(OFF_G, stage_g)
        return carry

    lax.fori_loop(0, N + OFF_G, step, 0)

    last = remote(acc.at[second], igz, gz_s, gz_r, partner)
    last.start()
    for copy in [to_partner, own_sib, pair_sib] + w_sib:
        copy.wait_send()
    last.wait()
    ig_o[...] = (acc[:OWN] + igz[...]).astype(BF16)
    done = pltpu.make_async_copy(ig_o, ig_out, outs.at[6])
    done.start()
    for copy in results():
        copy.wait()
    done.wait()


def local(inputs, cotangent, gate_weight, up_weight, down_weight):
    dma = pltpu.SemaphoreType.DMA
    anywhere = pl.BlockSpec(memory_space=pl.ANY)
    return pl.pallas_call(
        kernel,
        name="ffn_backward",
        out_shape=[
            jax.ShapeDtypeStruct((OWN, D), BF16),
            jax.ShapeDtypeStruct((D, F), BF16),
            jax.ShapeDtypeStruct((D, F), BF16),
            jax.ShapeDtypeStruct((F, D), BF16),
        ],
        in_specs=[anywhere] * 5,
        out_specs=[anywhere] * 4,
        scratch_shapes=[
            pltpu.VMEM((2, 2, N * TC, D), BF16),
            pltpu.VMEM((3, D, 2 * FH), BF16),
            pltpu.VMEM((3, FH, D), BF16),
            pltpu.VMEM((N * TC, W3), F32),
            pltpu.VMEM((N, Q, W3), BF16),
            pltpu.VMEM((N, Q, W3), BF16),
            pltpu.VMEM((N, 2, Q, W3), BF16),
            pltpu.VMEM((N, 2, Q, W3), BF16),
            pltpu.VMEM((2, N * TC, W3), BF16),
            pltpu.VMEM((N, TC, D), BF16),
            pltpu.VMEM((N, TC, D), BF16),
            pltpu.VMEM((TC, D), F32),
            pltpu.VMEM((OWN, D), F32),
            pltpu.VMEM((2, D, 2 * FH), F32),
            pltpu.VMEM((2, FH, D), F32),
            pltpu.VMEM((2, D, 2 * FH), BF16),
            pltpu.VMEM((2, FH, D), BF16),
            pltpu.VMEM((OWN, D), BF16),
            dma((8,)),
            dma(()), dma(()),
            dma((2,)), dma((2,)),
            dma((N + 1,)), dma((N + 1,)),
            dma((N,)), dma((N,)),
            dma((N, 2)), dma((N, 2)),
            dma((N, 2)), dma((N, 2)),
            dma((N, 2)), dma((N, 2)),
            dma((N, 2)), dma((N, 2)),
            dma((N,)), dma((N,)),
            dma((N,)), dma((N,)),
            dma(()), dma(()),
            dma((7,)),
        ],
        compiler_params=pltpu.CompilerParams(
            collective_id=0, has_side_effects=True, vmem_limit_bytes=40 * 2**20
        ),
    )(inputs, cotangent, gate_weight, up_weight, down_weight)


def solution(mesh):
    in_specs = (P("gy", "gx"), P("gy", "gx"), P("gx", "gy"), P("gx", "gy"), P("gy", "gx"))
    out_specs = (P("gy", "gx"), P("gx", "gy"), P("gx", "gy"), P("gy", "gx"))
    return jax.shard_map(local, mesh=mesh, in_specs=in_specs, out_specs=out_specs, check_vma=False)
```

time: 658 us -> 112 us (0.17)
  the two profiles are of different devices: /device:TPU:2 before, /device:TPU:40 now
where the time goes in v1:
time: 112 us
  Pallas kernels  104 us (93%)
  local copies, waits for them, and re-layouts  7.63 us (7%)
    pallas_call x1, Pallas kernels, local(): pl.pallas_call(kernel, name='ffn_backward', out_shape=[jax.ShapeDtypeStru...  104 us
    unnamed x14, local copies, waits for them, and re-layouts  7.63 us

profile of v1, /device:TPU:40, one launch (start us, length us, event | category | flops | bytes accessed | tf_op | source)
XLA Modules:
  0.0 112.1 jit_solution(12203369997181968123)
XLA Ops:
  0.6 0.0 copy-start
  0.6 1.0 copy-done
  1.7 0.0 copy-start.1
  1.7 1.0 copy-done.1
  2.7 0.0 copy-start.2
  2.7 1.0 copy-done.2
  3.8 0.0 copy-start.3
  3.8 0.8 copy-done.3
  4.5 0.0 copy-start.4
  4.5 0.8 copy-done.4
  5.3 103.8 %ffn_backward.1 = (bf16[32,512]{1,0:T(8,128)(2,1)S(1)}, bf16[512,512]{1,0:T(8,128)(2,1)S(1)}, bf16[512,512]{1,0:T(8,128)(2,1)S(1)}, bf16[512,512]{1,0:T(8,128)(2,1)S(1)}) custom-call(bf16[32,512]{1,0:T(8,128)(2,1)S(1)} %copy-done.3, bf16[32,512]{1,0:T(8,128)(2,1)S(1)} %copy-done.4, bf16[512,512]{1,0:T(8,128)(2,1)S(1)} %copy-done, ...), custom_call_target="tpu_custom_call" | custom-call | tf_op jit(solution)/shard_map/ffn_backward/pallas_call | solution.py:306
  109.1 0.6 copy.13
  109.7 0.8 copy.14
  110.5 0.8 copy.15
  111.3 0.8 copy.16
Async XLA Ops:
  0.6 1.0 copy-start
  1.7 1.0 copy-start.1
  2.7 1.0 copy-start.2
  3.8 0.8 copy-start.3
  4.5 0.8 copy-start.4

commit v2 on v1

--- a/solution.py
+++ b/solution.py
@@ -19,7 +19,24 @@
 W3 = 3 * FH
 WH = W3 // 2
 GROUP = 4
-OFF_B, OFF_C, OFF_D, OFF_E, OFF_F, OFF_G = 2, 4, 6, 8, 9, 11
+OWN_K = N - 1
+OFF_B, OFF_C, OFF_D, OFF_E, OFF_F, OFF_G = 2, 5, 7, 9, 10, 12
+
+
+def distance(i):
+    return jnp.where(i == 0, 1, jnp.where(i == 1, 3, 2))
+
+
+def far_pair(k):
+    e = (k - 5) % 9
+    return e // 3, e % 3
+
+
+def offset(k):
+    i, j = far_pair(k)
+    dy = jnp.where(k < 6, (k % 2) * distance(k // 2), distance(i))
+    dx = jnp.where(k < 6, (1 - k % 2) * distance(k // 2), distance(j))
+    return dy, dx
 
 
 def dot(a, b, dims):
@@ -41,7 +58,7 @@
     x_in, cot_in, wg_in, wu_in, wd_in,
     ig_out, gg_out, ug_out, dg_out,
     tok, wgu, wd, part, s1, r1, s2, r2, hid, igs, igr, acc, igz, gu, dn, gu_o, dn_o, ig_o,
-    loc, zl_s, zl_r, wx_s, wx_r, sx_s, sx_r, xs, xr, r1s, r1r, r2s, r2r, a1s, a1r, a2s, a2r, hs, hr, gs, gr, gz_s, gz_r, outs,
+    loc, zl_s, zl_r, wx_s, wx_r, sx_s, sx_r, xs, xr, cs, cr, r1s, r1r, r2s, r2r, a1s, a1r, a2s, a2r, hs, hr, gs, gr, gz_s, gz_r, outs,
 ):
     gx, gy = lax.axis_index("gx"), lax.axis_index("gy")
     zh, core = gx // 2, gx % 2
@@ -55,6 +72,7 @@
 
     sibling = (zh * 2 + 1 - core, gy)
     partner = (gx, (1 - zl) * 16 + y * 4 + x)
+    across_partner = (zh * 2 + 1 - core, (1 - zl) * 16 + y * 4 + x)
 
     def remote(src, dst, send, recv, device):
         return pltpu.make_async_remote_copy(
@@ -62,14 +80,14 @@
         )
 
     barrier = pltpu.get_barrier_semaphore()
-    for device in [ring(1), ring(-1), sibling, partner] + [plane(r // 4, r % 4) for r in range(1, N)]:
+    for device in [ring(1), ring(-1), sibling, partner, across_partner] + [plane(r // 4, r % 4) for r in range(1, N)]:
         pl.semaphore_signal(barrier, inc=1, device_id=device, device_id_type=MESH)
 
     mine = pl.ds(pl.multiple_of(core * FH, FH), FH)
     other = pl.ds(pl.multiple_of((1 - core) * FH, FH), FH)
     loads = [
-        (x_in, tok.at[0, 0, pl.ds(0, OWN)]),
-        (cot_in, tok.at[0, 1, pl.ds(0, OWN)]),
+        (x_in, tok.at[0, 0, pl.ds(OWN_K * TC, OWN)]),
+        (cot_in, tok.at[0, 1, pl.ds(OWN_K * TC, OWN)]),
         (wg_in.at[:, other], wgu.at[1, :, pl.ds(0, FH)]),
         (wu_in.at[:, other], wgu.at[1, :, pl.ds(FH, FH)]),
         (wd_in.at[other], wd.at[1]),
@@ -82,39 +100,55 @@
         load.start()
     gu[...] = jnp.zeros_like(gu)
     dn[...] = jnp.zeros_like(dn)
+    acc[...] = jnp.zeros_like(acc)
     for load in loads:
         load.wait()
-    pl.semaphore_wait(barrier, 4 + N - 1)
-
-    first, second = pl.ds(0, OWN), pl.ds(OWN, OWN)
-    to_partner = remote(tok.at[0, :, first], tok.at[0, :, second], zl_s, zl_r, partner)
-    to_partner.start()
-    own_sib = remote(tok.at[0, :, first], tok.at[1, :, first], sx_s.at[N], sx_r.at[N], sibling)
-    own_sib.start()
-    w_sib = [
+    pl.semaphore_wait(barrier, 5 + N - 1)
+
+    first, second = pl.ds(OWN_K * TC, OWN), pl.ds(OWN_K * TC + OWN, OWN)
+    own = tok.at[0, :, first]
+    firsts = [
+        remote(own, tok.at[0, :, second], zl_s.at[0], zl_r.at[0], partner),
+        remote(own, tok.at[1, :, second], zl_s.at[1], zl_r.at[1], across_partner),
+        remote(own, tok.at[1, :, first], sx_s.at[OWN_K], sx_r.at[OWN_K], sibling),
         remote(wgu.at[1], wgu.at[2], wx_s.at[0], wx_r.at[0], sibling),
         remote(wd.at[1], wd.at[2], wx_s.at[1], wx_r.at[1], sibling),
     ]
-    for copy in w_sib:
+    for copy in firsts:
         copy.start()
-    to_partner.wait_recv()
-    pair_sib = remote(tok.at[0, :, second], tok.at[1, :, second], sx_s.at[0], sx_r.at[0], sibling)
-    pair_sib.start()
 
     def rows(k):
         return pl.ds(pl.multiple_of(k * TC, TC), TC)
 
     def spread(k):
-        return remote(tok.at[0, :, pl.ds(0, TC)], tok.at[0, :, rows(k)], xs.at[k], xr.at[k], plane(k // 4, k % 4))
-
-    def start_spread(k, carry):
-        spread(k).start()
-        return carry
-
-    lax.fori_loop(1, N, start_spread, 0)
+        to = plane(*offset(k))
+        return [
+            remote(
+                tok.at[0, :, part_of], tok.at[0, :, pl.ds(pl.multiple_of(k * TC + h * OWN, OWN), OWN)],
+                xs.at[k], xr.at[k], to,
+            ) if h == 0 else remote(
+                tok.at[0, :, part_of], tok.at[0, :, pl.ds(pl.multiple_of(k * TC + h * OWN, OWN), OWN)],
+                cs.at[k], cr.at[k], to,
+            )
+            for h, part_of in enumerate((first, second))
+        ]
+
+    def spread_x(k):
+        i, j = far_pair(k)
+        return remote(tok.at[0, 0, rows(2 * j)], tok.at[0, 0, rows(k)], xs.at[k], xr.at[k], plane(distance(i), 0))
+
+    def spread_c(k):
+        i, j = far_pair(k)
+        return remote(tok.at[0, 1, rows(2 * i + 1)], tok.at[0, 1, rows(k)], cs.at[k], cr.at[k], plane(0, distance(j)))
 
     def forward(k):
         return remote(tok.at[0, :, rows(k)], tok.at[1, :, rows(k)], sx_s.at[k], sx_r.at[k], sibling)
+
+    for k in range(6):
+        spread(k)[0].start()
+    firsts[0].wait_recv()
+    for k in range(6):
+        spread(k)[1].start()
 
     lo, hi = pl.ds(0, WH), pl.ds(WH, WH)
 
@@ -151,23 +185,35 @@
         return remote(hid.at[0, rows(k)], hid.at[1, rows(k)], hs.at[k], hr.at[k], sibling)
 
     def give(k):
-        return remote(igs.at[k], igr.at[k], gs.at[k], gr.at[k], plane(-(k // 4), -(k % 4)))
-
-    def stage_x(k):
-        @pl.when(k > 0)
-        def _():
-            spread(k).wait_recv()
-            forward(k).start()
+        return remote(igs.at[k], igr.at[k], gs.at[k], gr.at[k], plane(-offset(k)[0], -offset(k)[1]))
+
+    def far(i, j):
+        return 6 + (3 * i + j + 8) % 9
+
+    def stage_near(i):
+        for copy in spread(2 * i):
+            copy.wait_recv()
+        for other_i in range(3):
+            spread_x(far(other_i, i)).start()
+        forward(2 * i).start()
+        for copy in spread(2 * i + 1):
+            copy.wait_recv()
+        for other_i in range(3):
+            spread_c(far(i, other_i)).start()
+        forward(2 * i + 1).start()
+
+    def stage_far(k):
+        spread_x(k).wait_recv()
+        spread_c(k).wait_recv()
+        forward(k).start()
 
     def stage_a(k):
-        @pl.when(k == 0)
-        def _():
-            own_sib.wait_recv()
-            pair_sib.wait_recv()
-            for copy in w_sib:
+        @pl.when(k == OWN_K)
+        def _():
+            for copy in firsts[1:]:
                 copy.wait_recv()
 
-        @pl.when(k > 0)
+        @pl.when(k < OWN_K)
         def _():
             forward(k).wait_recv()
 
@@ -221,11 +267,11 @@
         back = ((1,), (1,))
         share = dot(hid[0, here, FH:], wgu[0], back) + dot(hid[1, here, FH:], wgu[1], back)
 
-        @pl.when(k == 0)
-        def _():
-            acc[...] = share
-
-        @pl.when(k > 0)
+        @pl.when(k == OWN_K)
+        def _():
+            acc[...] += share
+
+        @pl.when(k < OWN_K)
         def _():
             igs[k] = share.astype(BF16)
             give(k).start()
@@ -256,40 +302,57 @@
         return [pltpu.make_async_copy(src, dst, outs.at[i]) for i, (src, dst) in enumerate(copies)]
 
     def stage_g(k):
-        @pl.when(k > 0)
+        @pl.when(k < OWN_K)
         def _():
             give(k).wait_recv()
             acc[...] += igr[k].astype(F32)
             give(k).wait_send()
-            spread(k).wait_send()
             forward(k).wait_send()
+
+        @pl.when(k < 6)
+        def _():
+            for copy in spread(k):
+                copy.wait_send()
+
+        @pl.when(jnp.logical_and(k >= 6, k < OWN_K))
+        def _():
+            spread_x(k).wait_send()
+            spread_c(k).wait_send()
 
         for copy in reduce1(k) + reduce2(k) + gather1(k, 0) + gather2(k, -1, 1) + (across(k),):
             copy.wait_send()
 
     def step(s, carry):
-        def at(offset, stage):
-            k = s - offset
+        def at(off, stage, turn=0):
+            k = s - off
 
             @pl.when(jnp.logical_and(k >= 0, k < N))
             def _():
-                stage(k)
-
-        at(0, stage_x)
-        at(OFF_B, stage_b)
+                stage((k + turn) % N)
+
+        at(0, stage_a, N - 1)
+
+        @pl.when(s < 3)
+        def _():
+            stage_near(s)
+
+        @pl.when(jnp.logical_and(s >= 3, s < N - 4))
+        def _():
+            stage_far(s + 3)
+
+        at(OFF_B, stage_b, N - 1)
         at(OFF_C, stage_c)
         at(OFF_D, stage_d)
         at(OFF_E, stage_e)
-        at(0, stage_a)
         at(OFF_F, stage_f)
         at(OFF_G, stage_g)
         return carry
 
     lax.fori_loop(0, N + OFF_G, step, 0)
 
-    last = remote(acc.at[second], igz, gz_s, gz_r, partner)
+    last = remote(acc.at[pl.ds(OWN, OWN)], igz, gz_s, gz_r, partner)
     last.start()
-    for copy in [to_partner, own_sib, pair_sib] + w_sib:
+    for copy in firsts:
         copy.wait_send()
     last.wait()
     ig_o[...] = (acc[:OWN] + igz[...]).astype(BF16)
@@ -300,10 +363,23 @@
     done.wait()
 
 
+def publish(*refs):
+    given, taken, held, sems = refs[:4], refs[4:8], refs[8:12], refs[12]
+    loads = [pltpu.make_async_copy(given[i], held[i], sems.at[i]) for i in range(4)]
+    stores = [pltpu.make_async_copy(held[i], taken[i], sems.at[4 + i]) for i in range(4)]
+    for load in loads:
+        load.start()
+    for load, store in zip(loads, stores):
+        load.wait()
+        store.start()
+    for store in stores:
+        store.wait()
+
+
 def local(inputs, cotangent, gate_weight, up_weight, down_weight):
     dma = pltpu.SemaphoreType.DMA
     anywhere = pl.BlockSpec(memory_space=pl.ANY)
-    return pl.pallas_call(
+    results = pl.pallas_call(
         kernel,
         name="ffn_backward",
         out_shape=[
@@ -334,9 +410,10 @@
             pltpu.VMEM((2, FH, D), BF16),
             pltpu.VMEM((OWN, D), BF16),
             dma((8,)),
-            dma(()), dma(()),
+            dma((2,)), dma((2,)),
             dma((2,)), dma((2,)),
             dma((N + 1,)), dma((N + 1,)),
+            dma((N,)), dma((N,)),
             dma((N,)), dma((N,)),
             dma((N, 2)), dma((N, 2)),
             dma((N, 2)), dma((N, 2)),
@@ -348,9 +425,17 @@
             dma((7,)),
         ],
         compiler_params=pltpu.CompilerParams(
-            collective_id=0, has_side_effects=True, vmem_limit_bytes=40 * 2**20
+            collective_id=0, has_side_effects=True, vmem_limit_bytes=60 * 2**20
         ),
     )(inputs, cotangent, gate_weight, up_weight, down_weight)
+    return pl.pallas_call(
+        publish,
+        name="publish",
+        out_shape=[jax.ShapeDtypeStruct(result.shape, BF16) for result in results],
+        in_specs=[anywhere] * 4,
+        out_specs=[anywhere] * 4,
+        scratch_shapes=[pltpu.VMEM(result.shape, BF16) for result in results] + [dma((8,))],
+    )(*results)
 
 
 def solution(mesh):

time: 112 us -> 93.9 us (0.84)
  the two profiles are of different devices: /device:TPU:40 before, /device:TPU:2 now
where the time goes in v2:
time: 93.9 us; the launch traced here: 93.8 us
  Pallas kernels  93.2 us (99%)
    pallas_call x1, Pallas kernels, local(): pl.pallas_call(kernel, name='ffn_backward', out_shape=[jax.ShapeDtypeStru...  90.9 us
    pallas_call x1, Pallas kernels, local(): pl.pallas_call(publish, name='publish', out_shape=[jax.ShapeDtypeStruct(r...  2.27 us

profile of v2, /device:TPU:2, one launch (start us, length us, event | category | flops | bytes accessed | tf_op | source)
XLA Modules:
  0.0 93.8 jit_solution(15143477995005639881)
XLA Ops:
  0.6 90.9 %ffn_backward.1 = (bf16[32,512]{1,0:T(8,128)(2,1)}, bf16[512,512]{1,0:T(8,128)(2,1)}, bf16[512,512]{1,0:T(8,128)(2,1)}, bf16[512,512]{1,0:T(8,128)(2,1)}) custom-call(bf16[32,512]{1,0:T(8,128)(2,1)} %x_in.1, bf16[32,512]{1,0:T(8,128)(2,1)} %cot_in.1, bf16[512,512]{1,0:T(8,128)(2,1)} %wg_in.1, bf16[512,512]{1,0:T(8,128)(2,1)} %wu_in.1, bf16[512,512]{1,0:T(8,128)(2,1)} %wd_in.1), custom_call_target="tpu_custom_call" | custom-call | tf_op jit(solution)/shard_map/ffn_backward/pallas_call | solution.py:382
  91.5 2.3 %publish.1 = (bf16[32,512]{1,0:T(8,128)(2,1)}, bf16[512,512]{1,0:T(8,128)(2,1)}, bf16[512,512]{1,0:T(8,128)(2,1)}, bf16[512,512]{1,0:T(8,128)(2,1)}) custom-call(bf16[32,512]{1,0:T(8,128)(2,1)} %get-tuple-element.8.refs_0_, bf16[512,512]{1,0:T(8,128)(2,1)} %get-tuple-element.9.refs_1_, bf16[512,512]{1,0:T(8,128)(2,1)} %get-tuple-element.10.refs_2_, ...), custom_call_target="tpu_custom_call" | custom-call | tf_op jit(solution)/shard_map/publish/pallas_call | solution.py:431

commit v3 on v2

--- a/solution.py
+++ b/solution.py
@@ -19,24 +19,16 @@
 W3 = 3 * FH
 WH = W3 // 2
 GROUP = 4
+DIRECT = 12
 OWN_K = N - 1
-OFF_B, OFF_C, OFF_D, OFF_E, OFF_F, OFF_G = 2, 5, 7, 9, 10, 12
-
-
-def distance(i):
-    return jnp.where(i == 0, 1, jnp.where(i == 1, 3, 2))
-
-
-def far_pair(k):
-    e = (k - 5) % 9
-    return e // 3, e % 3
-
-
-def offset(k):
-    i, j = far_pair(k)
-    dy = jnp.where(k < 6, (k % 2) * distance(k // 2), distance(i))
-    dx = jnp.where(k < 6, (1 - k % 2) * distance(k // 2), distance(j))
-    return dy, dx
+OFF_B, OFF_C, OFF_D, OFF_E, OFF_F, OFF_G = 3, 7, 10, 13, 14, 17
+
+
+DISTANCE = (1, 3, 2)
+NEAR = [(0, d) if axis == 0 else (d, 0) for d in DISTANCE for axis in range(2)]
+FAR = [(i, j) for i in range(3) for j in range(3)]
+FAR = FAR[1:] + FAR[:1]
+OFFSET = NEAR + [(DISTANCE[i], DISTANCE[j]) for i, j in FAR] + [(0, 0)]
 
 
 def dot(a, b, dims):
@@ -57,18 +49,26 @@
 def kernel(
     x_in, cot_in, wg_in, wu_in, wd_in,
     ig_out, gg_out, ug_out, dg_out,
-    tok, wgu, wd, part, s1, r1, s2, r2, hid, igs, igr, acc, igz, gu, dn, gu_o, dn_o, ig_o,
-    loc, zl_s, zl_r, wx_s, wx_r, sx_s, sx_r, xs, xr, cs, cr, r1s, r1r, r2s, r2r, a1s, a1r, a2s, a2r, hs, hr, gs, gr, gz_s, gz_r, outs,
+    tok, wgu, wd, part, s1, r1, s2, r2, hid, igs, igr, acc, igz, own_share, gu, dn,
+    loc, zl_s, zl_r, wx_s, wx_r, sx_s, sx_r, xs, xr, cs, cr, r1s, r1r, r2s, r2r, a1s, a1r, a2s, a2r, hs, hr, gs, gr, gs2, gr2, gz_s, gz_r,
 ):
     gx, gy = lax.axis_index("gx"), lax.axis_index("gy")
     zh, core = gx // 2, gx % 2
     zl, y, x = gy // 16, (gy // 4) % 4, gy % 4
 
+    z_at = [(zh + i) % 4 for i in range(4)]
+    y_at = [zl * 16 + ((y + i) % 4) * 4 for i in range(4)]
+    x_at = [(x + i) % 4 for i in range(4)]
+    ring_at = [(z_at[i] * 2 + core, gy) for i in range(4)]
+
     def ring(step):
-        return (((zh + step + 4) % 4) * 2 + core, gy)
+        return ring_at[step % 4]
 
     def plane(dy, dx):
-        return (gx, zl * 16 + ((y + dy + 4) % 4) * 4 + (x + dx + 4) % 4)
+        return (gx, y_at[dy % 4] + x_at[dx % 4])
+
+    def other_plane(dy, dx):
+        return (gx, y_at[dy % 4] + x_at[dx % 4] + 16 - 32 * zl)
 
     sibling = (zh * 2 + 1 - core, gy)
     partner = (gx, (1 - zl) * 16 + y * 4 + x)
@@ -80,7 +80,9 @@
         )
 
     barrier = pltpu.get_barrier_semaphore()
-    for device in [ring(1), ring(-1), sibling, partner, across_partner] + [plane(r // 4, r % 4) for r in range(1, N)]:
+    for device in [ring(1), ring(-1), sibling, partner, across_partner] + [plane(*o) for o in OFFSET[:OWN_K]] + [
+        other_plane(*o) for o in OFFSET[DIRECT:OWN_K]
+    ]:
         pl.semaphore_signal(barrier, inc=1, device_id=device, device_id_type=MESH)
 
     mine = pl.ds(pl.multiple_of(core * FH, FH), FH)
@@ -103,7 +105,7 @@
     acc[...] = jnp.zeros_like(acc)
     for load in loads:
         load.wait()
-    pl.semaphore_wait(barrier, 5 + N - 1)
+    pl.semaphore_wait(barrier, 5 + N - 1 + OWN_K - DIRECT)
 
     first, second = pl.ds(OWN_K * TC, OWN), pl.ds(OWN_K * TC + OWN, OWN)
     own = tok.at[0, :, first]
@@ -120,40 +122,32 @@
     def rows(k):
         return pl.ds(pl.multiple_of(k * TC, TC), TC)
 
-    def spread(k):
-        to = plane(*offset(k))
+    def spread(k, to=(0, 0)):
+        here = [pl.ds(pl.multiple_of(k * TC + h * OWN, OWN), OWN) for h in range(2)]
         return [
-            remote(
-                tok.at[0, :, part_of], tok.at[0, :, pl.ds(pl.multiple_of(k * TC + h * OWN, OWN), OWN)],
-                xs.at[k], xr.at[k], to,
-            ) if h == 0 else remote(
-                tok.at[0, :, part_of], tok.at[0, :, pl.ds(pl.multiple_of(k * TC + h * OWN, OWN), OWN)],
-                cs.at[k], cr.at[k], to,
-            )
-            for h, part_of in enumerate((first, second))
+            remote(tok.at[0, :, first], tok.at[0, :, here[0]], xs.at[k], xr.at[k], plane(*to)),
+            remote(tok.at[0, :, second], tok.at[0, :, here[1]], cs.at[k], cr.at[k], plane(*to)),
         ]
 
-    def spread_x(k):
-        i, j = far_pair(k)
-        return remote(tok.at[0, 0, rows(2 * j)], tok.at[0, 0, rows(k)], xs.at[k], xr.at[k], plane(distance(i), 0))
-
-    def spread_c(k):
-        i, j = far_pair(k)
-        return remote(tok.at[0, 1, rows(2 * i + 1)], tok.at[0, 1, rows(k)], cs.at[k], cr.at[k], plane(0, distance(j)))
+    def spread_x(k, i=0, j=0):
+        return remote(tok.at[0, 0, rows(2 * j)], tok.at[0, 0, rows(k)], xs.at[k], xr.at[k], plane(DISTANCE[i], 0))
+
+    def spread_c(k, i=0, j=0):
+        return remote(tok.at[0, 1, rows(2 * i + 1)], tok.at[0, 1, rows(k)], cs.at[k], cr.at[k], plane(0, DISTANCE[j]))
 
     def forward(k):
         return remote(tok.at[0, :, rows(k)], tok.at[1, :, rows(k)], sx_s.at[k], sx_r.at[k], sibling)
 
     for k in range(6):
-        spread(k)[0].start()
+        spread(k, OFFSET[k])[0].start()
     firsts[0].wait_recv()
     for k in range(6):
-        spread(k)[1].start()
+        spread(k, OFFSET[k])[1].start()
 
     lo, hi = pl.ds(0, WH), pl.ds(WH, WH)
 
     def quarter(k, step):
-        return pl.ds(pl.multiple_of(k * TC + ((zh + step + 4) % 4) * Q, Q), Q)
+        return pl.ds(pl.multiple_of(k * TC + z_at[step % 4] * Q, Q), Q)
 
     def reduce1(k):
         return (
@@ -184,23 +178,39 @@
     def across(k):
         return remote(hid.at[0, rows(k)], hid.at[1, rows(k)], hs.at[k], hr.at[k], sibling)
 
+    def select(k, ids, low, high):
+        to = ids[low]
+        for i in range(low + 1, high):
+            to = jnp.where(k == i, ids[i], to)
+        return to
+
+    owner = [plane(-dy, -dx)[1] for dy, dx in OFFSET]
+    other_owner = [other_plane(-dy, -dx)[1] for dy, dx in OFFSET]
+    up_rows, down_rows = pl.ds(0, OWN), pl.ds(OWN, OWN)
+
     def give(k):
-        return remote(igs.at[k], igr.at[k], gs.at[k], gr.at[k], plane(-offset(k)[0], -offset(k)[1]))
-
-    def far(i, j):
-        return 6 + (3 * i + j + 8) % 9
+        return remote(igs.at[k], igr.at[k], gs.at[k], gr.at[k], (gx, select(k, owner, 0, DIRECT)))
+
+    def give_direct(k):
+        here, there = select(k, owner, DIRECT, OWN_K), select(k, other_owner, DIRECT, N)
+        return [
+            remote(igs.at[k, up_rows], igr.at[k, up_rows], gs.at[k], gr.at[k], (gx, here)),
+            remote(igs.at[k, down_rows], igr.at[k, down_rows], gs2.at[k], gr2.at[k], (gx, there)),
+        ]
+
+    def exchange():
+        return remote(acc.at[down_rows], igz, gz_s, gz_r, partner)
 
     def stage_near(i):
-        for copy in spread(2 * i):
-            copy.wait_recv()
-        for other_i in range(3):
-            spread_x(far(other_i, i)).start()
-        forward(2 * i).start()
-        for copy in spread(2 * i + 1):
-            copy.wait_recv()
-        for other_i in range(3):
-            spread_c(far(i, other_i)).start()
-        forward(2 * i + 1).start()
+        for k in (2 * i, 2 * i + 1):
+            for copy in spread(k):
+                copy.wait_recv()
+            for n, (a, b) in enumerate(FAR):
+                if k == 2 * b:
+                    spread_x(6 + n, a, b).start()
+                if k == 2 * a + 1:
+                    spread_c(6 + n, a, b).start()
+            forward(k).start()
 
     def stage_far(k):
         spread_x(k).wait_recv()
@@ -267,18 +277,25 @@
         back = ((1,), (1,))
         share = dot(hid[0, here, FH:], wgu[0], back) + dot(hid[1, here, FH:], wgu[1], back)
 
+        igs[k] = share.astype(BF16)
+
+        @pl.when(k < DIRECT)
+        def _():
+            give(k).start()
+
+        @pl.when(jnp.logical_and(k >= DIRECT, k < OWN_K))
+        def _():
+            for copy in give_direct(k):
+                copy.start()
+
         @pl.when(k == OWN_K)
         def _():
-            acc[...] += share
-
-        @pl.when(k < OWN_K)
-        def _():
-            igs[k] = share.astype(BF16)
-            give(k).start()
-
-        @pl.when(k % GROUP == GROUP - 1)
-        def _():
-            block = pl.ds(pl.multiple_of((k // GROUP) * GROUP * TC, GROUP * TC), GROUP * TC)
+            own_share[...] = share[:OWN]
+            give_direct(k)[1].start()
+
+        @pl.when(functools.reduce(jnp.logical_or, [k == i for i in range(GROUP - 1, N, GROUP)]))
+        def _():
+            block = pl.ds(pl.multiple_of((k - (GROUP - 1)) * TC, GROUP * TC), GROUP * TC)
             over = ((0,), (0,))
             for h in range(2):
                 gu[h] += dot(tok[0, 0, block], hid[h, block, FH:], over)
@@ -286,27 +303,29 @@
 
         @pl.when(k == N - 1)
         def _():
-            gu_o[...] = gu[...].astype(BF16)
-            dn_o[...] = dn[...].astype(BF16)
-            for copy in results():
-                copy.start()
-
-    def results():
-        copies = []
-        for h, cols in enumerate((mine, other)):
-            copies += [
-                (gu_o.at[h, :, pl.ds(0, FH)], gg_out.at[:, cols]),
-                (gu_o.at[h, :, pl.ds(FH, FH)], ug_out.at[:, cols]),
-                (dn_o.at[h], dg_out.at[cols]),
-            ]
-        return [pltpu.make_async_copy(src, dst, outs.at[i]) for i, (src, dst) in enumerate(copies)]
+            for h, cols in enumerate((mine, other)):
+                gg_out[:, cols] = gu[h, :, :FH].astype(BF16)
+                ug_out[:, cols] = gu[h, :, FH:].astype(BF16)
+                dg_out[cols, :] = dn[h].astype(BF16)
 
     def stage_g(k):
-        @pl.when(k < OWN_K)
+        @pl.when(k < DIRECT)
         def _():
             give(k).wait_recv()
             acc[...] += igr[k].astype(F32)
             give(k).wait_send()
+
+        @pl.when(k == DIRECT - 1)
+        def _():
+            exchange().start()
+
+        @pl.when(jnp.logical_and(k >= DIRECT, k < OWN_K))
+        def _():
+            for copy in give_direct(k):
+                copy.wait_send()
+
+        @pl.when(k < OWN_K)
+        def _():
             forward(k).wait_send()
 
         @pl.when(k < 6)
@@ -323,24 +342,22 @@
             copy.wait_send()
 
     def step(s, carry):
-        def at(off, stage, turn=0):
+        def at(off, stage, own_first=False):
             k = s - off
 
             @pl.when(jnp.logical_and(k >= 0, k < N))
             def _():
-                stage((k + turn) % N)
-
-        at(0, stage_a, N - 1)
-
-        @pl.when(s < 3)
-        def _():
-            stage_near(s)
-
-        @pl.when(jnp.logical_and(s >= 3, s < N - 4))
-        def _():
-            stage_far(s + 3)
-
-        at(OFF_B, stage_b, N - 1)
+                stage(jnp.where(k == 0, OWN_K, k - 1) if own_first else k)
+
+        at(0, stage_a, True)
+        for i in range(3):
+            pl.when(s == i)(functools.partial(stage_near, i))
+
+        @pl.when(jnp.logical_and(s >= 5, s < N - 1 - 1))
+        def _():
+            stage_far(s + 1)
+
+        at(OFF_B, stage_b, True)
         at(OFF_C, stage_c)
         at(OFF_D, stage_d)
         at(OFF_E, stage_e)
@@ -350,46 +367,45 @@
 
     lax.fori_loop(0, N + OFF_G, step, 0)
 
-    last = remote(acc.at[pl.ds(OWN, OWN)], igz, gz_s, gz_r, partner)
-    last.start()
     for copy in firsts:
         copy.wait_send()
-    last.wait()
-    ig_o[...] = (acc[:OWN] + igz[...]).astype(BF16)
-    done = pltpu.make_async_copy(ig_o, ig_out, outs.at[6])
-    done.start()
-    for copy in results():
+    exchange().wait()
+    total = acc[:OWN] + own_share[...] + igz[...]
+    for k in range(DIRECT, OWN_K):
+        for copy in give_direct(k):
+            copy.wait_recv()
+        total += igr[k, :OWN].astype(F32) + igr[k, OWN:].astype(F32)
+    give_direct(OWN_K)[1].wait()
+    ig_out[...] = (total + igr[OWN_K, OWN:].astype(F32)).astype(BF16)
+
+
+def publish(*refs):
+    sems = refs[8]
+    copies = [pltpu.make_async_copy(refs[i], refs[4 + i], sems.at[i]) for i in range(4)]
+    for copy in copies:
+        copy.start()
+    for copy in copies:
         copy.wait()
-    done.wait()
-
-
-def publish(*refs):
-    given, taken, held, sems = refs[:4], refs[4:8], refs[8:12], refs[12]
-    loads = [pltpu.make_async_copy(given[i], held[i], sems.at[i]) for i in range(4)]
-    stores = [pltpu.make_async_copy(held[i], taken[i], sems.at[4 + i]) for i in range(4)]
-    for load in loads:
-        load.start()
-    for load, store in zip(loads, stores):
-        load.wait()
-        store.start()
-    for store in stores:
-        store.wait()
 
 
 def local(inputs, cotangent, gate_weight, up_weight, down_weight):
     dma = pltpu.SemaphoreType.DMA
+    operands = [
+        pltpu.with_memory_space_constraint(a, pltpu.HBM)
+        for a in (inputs, cotangent, gate_weight, up_weight, down_weight)
+    ]
     anywhere = pl.BlockSpec(memory_space=pl.ANY)
     results = pl.pallas_call(
         kernel,
         name="ffn_backward",
         out_shape=[
-            jax.ShapeDtypeStruct((OWN, D), BF16),
-            jax.ShapeDtypeStruct((D, F), BF16),
-            jax.ShapeDtypeStruct((D, F), BF16),
-            jax.ShapeDtypeStruct((F, D), BF16),
+            pltpu.VMEM((OWN, D), BF16),
+            pltpu.VMEM((D, F), BF16),
+            pltpu.VMEM((D, F), BF16),
+            pltpu.VMEM((F, D), BF16),
         ],
         in_specs=[anywhere] * 5,
-        out_specs=[anywhere] * 4,
+        out_specs=[pl.BlockSpec(memory_space=pltpu.VMEM)] * 4,
         scratch_shapes=[
             pltpu.VMEM((2, 2, N * TC, D), BF16),
             pltpu.VMEM((3, D, 2 * FH), BF16),
@@ -404,11 +420,9 @@
             pltpu.VMEM((N, TC, D), BF16),
             pltpu.VMEM((TC, D), F32),
             pltpu.VMEM((OWN, D), F32),
+            pltpu.VMEM((OWN, D), F32),
             pltpu.VMEM((2, D, 2 * FH), F32),
             pltpu.VMEM((2, FH, D), F32),
-            pltpu.VMEM((2, D, 2 * FH), BF16),
-            pltpu.VMEM((2, FH, D), BF16),
-            pltpu.VMEM((OWN, D), BF16),
             dma((8,)),
             dma((2,)), dma((2,)),
             dma((2,)), dma((2,)),
@@ -421,20 +435,21 @@
             dma((N, 2)), dma((N, 2)),
             dma((N,)), dma((N,)),
             dma((N,)), dma((N,)),
+            dma((N,)), dma((N,)),
             dma(()), dma(()),
-            dma((7,)),
         ],
         compiler_params=pltpu.CompilerParams(
-            collective_id=0, has_side_effects=True, vmem_limit_bytes=60 * 2**20
+            collective_id=0, has_side_effects=True, vmem_limit_bytes=48 * 2**20
         ),
-    )(inputs, cotangent, gate_weight, up_weight, down_weight)
+    )(*operands)
     return pl.pallas_call(
         publish,
         name="publish",
         out_shape=[jax.ShapeDtypeStruct(result.shape, BF16) for result in results],
         in_specs=[anywhere] * 4,
         out_specs=[anywhere] * 4,
-        scratch_shapes=[pltpu.VMEM(result.shape, BF16) for result in results] + [dma((8,))],
+        scratch_shapes=[dma((4,))],
+        compiler_params=pltpu.CompilerParams(vmem_limit_bytes=4 * 2**20),
     )(*results)
 
 

time: 93.9 us -> 88.9 us (0.947); the launches traced: 93.8 us -> 87.5 us
  Pallas kernels: 93.2 us -> 86.8 us
    pallas_call x1, Pallas kernels: 90.9 us -> 85.6 us  [local(): pl.pallas_call(kernel, name='ffn_backward', out_shape=[pltpu.VMEM((OWN, D...]
    pallas_call x1, Pallas kernels: 2.27 us -> 1.19 us  [local(): pl.pallas_call(publish, name='publish', out_shape=[jax.ShapeDtypeStruct(r...]
where the time goes in v3:
time: 88.9 us; the launch traced here: 87.5 us
  Pallas kernels  86.8 us (98%)
    pallas_call x1, Pallas kernels, local(): pl.pallas_call(kernel, name='ffn_backward', out_shape=[pltpu.VMEM((OWN, D...  85.6 us

profile of v3, /device:TPU:2, one launch (start us, length us, event | category | flops | bytes accessed | tf_op | source)
XLA Modules:
  0.0 87.5 jit_solution(729124211985375189)
XLA Ops:
  0.6 85.6 %ffn_backward.1 = (bf16[32,512]{1,0:T(8,128)(2,1)S(1)}, bf16[512,512]{1,0:T(8,128)(2,1)S(1)}, bf16[512,512]{1,0:T(8,128)(2,1)S(1)}, bf16[512,512]{1,0:T(8,128)(2,1)S(1)}) custom-call(bf16[32,512]{1,0:T(8,128)(2,1)} %x_in.1, bf16[32,512]{1,0:T(8,128)(2,1)} %cot_in.1, bf16[512,512]{1,0:T(8,128)(2,1)} %wg_in.1, bf16[512,512]{1,0:T(8,128)(2,1)} %wu_in.1, ...), custom_call_target="tpu_custom_call" | custom-call | tf_op jit(solution)/shard_map/ffn_backward/pallas_call | solution.py:398
  86.3 1.2 %publish.1 = (bf16[32,512]{1,0:T(8,128)(2,1)}, bf16[512,512]{1,0:T(8,128)(2,1)}, bf16[512,512]{1,0:T(8,128)(2,1)}, bf16[512,512]{1,0:T(8,128)(2,1)}) custom-call(bf16[32,512]{1,0:T(8,128)(2,1)S(1)} %get-tuple-element.8.refs_0_, bf16[512,512]{1,0:T(8,128)(2,1)S(1)} %get-tuple-element.9.refs_1_, bf16[512,512]{1,0:T(8,128)(2,1)S(1)} %get-tuple-element.10.refs_2_, ...), custom_call_target="tpu_custom_call" | custom-call | tf_op jit(solution)/shard_map/publish/pallas_call | solution.py:445

commit v4 on v3

--- a/solution.py
+++ b/solution.py
@@ -80,9 +80,7 @@
         )
 
     barrier = pltpu.get_barrier_semaphore()
-    for device in [ring(1), ring(-1), sibling, partner, across_partner] + [plane(*o) for o in OFFSET[:OWN_K]] + [
-        other_plane(*o) for o in OFFSET[DIRECT:OWN_K]
-    ]:
+    for device in [ring(1), ring(-1), sibling, partner, across_partner] + [plane(*o) for o in NEAR]:
         pl.semaphore_signal(barrier, inc=1, device_id=device, device_id_type=MESH)
 
     mine = pl.ds(pl.multiple_of(core * FH, FH), FH)
@@ -105,7 +103,7 @@
     acc[...] = jnp.zeros_like(acc)
     for load in loads:
         load.wait()
-    pl.semaphore_wait(barrier, 5 + N - 1 + OWN_K - DIRECT)
+    pl.semaphore_wait(barrier, 5 + len(NEAR))
 
     first, second = pl.ds(OWN_K * TC, OWN), pl.ds(OWN_K * TC + OWN, OWN)
     own = tok.at[0, :, first]

time: 88.9 us -> 88 us (0.990)
  no operation moved by 1% of the time
where the time goes in v4:
time: 88 us; the launch traced here: 87.2 us
  Pallas kernels  86.6 us (98%)
    pallas_call x1, Pallas kernels, local(): pl.pallas_call(kernel, name='ffn_backward', out_shape=[pltpu.VMEM((OWN, D...  85.4 us

profile of v4, /device:TPU:2, one launch (start us, length us, event | category | flops | bytes accessed | tf_op | source)
XLA Modules:
  0.0 87.2 jit_solution(1990451752698939787)
XLA Ops:
  0.6 85.4 %ffn_backward.1 = (bf16[32,512]{1,0:T(8,128)(2,1)S(1)}, bf16[512,512]{1,0:T(8,128)(2,1)S(1)}, bf16[512,512]{1,0:T(8,128)(2,1)S(1)}, bf16[512,512]{1,0:T(8,128)(2,1)S(1)}) custom-call(bf16[32,512]{1,0:T(8,128)(2,1)} %x_in.1, bf16[32,512]{1,0:T(8,128)(2,1)} %cot_in.1, bf16[512,512]{1,0:T(8,128)(2,1)} %wg_in.1, bf16[512,512]{1,0:T(8,128)(2,1)} %wu_in.1, ...), custom_call_target="tpu_custom_call" | custom-call | tf_op jit(solution)/shard_map/ffn_backward/pallas_call | solution.py:396
  86.1 1.2 %publish.1 = (bf16[32,512]{1,0:T(8,128)(2,1)}, bf16[512,512]{1,0:T(8,128)(2,1)}, bf16[512,512]{1,0:T(8,128)(2,1)}, bf16[512,512]{1,0:T(8,128)(2,1)}) custom-call(bf16[32,512]{1,0:T(8,128)(2,1)S(1)} %get-tuple-element.8.refs_0_, bf16[512,512]{1,0:T(8,128)(2,1)S(1)} %get-tuple-element.9.refs_1_, bf16[512,512]{1,0:T(8,128)(2,1)S(1)} %get-tuple-element.10.refs_2_, ...), custom_call_target="tpu_custom_call" | custom-call | tf_op jit(solution)/shard_map/publish/pallas_call | solution.py:443

commit v5 on v4

--- a/solution.py
+++ b/solution.py
@@ -98,10 +98,7 @@
     loads = [pltpu.make_async_copy(src, dst, loc.at[i]) for i, (src, dst) in enumerate(loads)]
     for load in loads:
         load.start()
-    gu[...] = jnp.zeros_like(gu)
-    dn[...] = jnp.zeros_like(dn)
-    acc[...] = jnp.zeros_like(acc)
-    for load in loads:
+    for load in loads[:2]:
         load.wait()
     pl.semaphore_wait(barrier, 5 + len(NEAR))
 
@@ -114,7 +111,7 @@
         remote(wgu.at[1], wgu.at[2], wx_s.at[0], wx_r.at[0], sibling),
         remote(wd.at[1], wd.at[2], wx_s.at[1], wx_r.at[1], sibling),
     ]
-    for copy in firsts:
+    for copy in firsts[:3]:
         copy.start()
 
     def rows(k):
@@ -138,6 +135,13 @@
 
     for k in range(6):
         spread(k, OFFSET[k])[0].start()
+    for load in loads[2:]:
+        load.wait()
+    for copy in firsts[3:]:
+        copy.start()
+    gu[...] = jnp.zeros_like(gu)
+    dn[...] = jnp.zeros_like(dn)
+    acc[...] = jnp.zeros_like(acc)
     firsts[0].wait_recv()
     for k in range(6):
         spread(k, OFFSET[k])[1].start()

time: 88 us -> 87.7 us (level)
  no operation moved by 1% of the time
where the time goes in v5:
time: 87.7 us; the launch traced here: 87.1 us
  Pallas kernels  86.5 us (99%)
    pallas_call x1, Pallas kernels, local(): pl.pallas_call(kernel, name='ffn_backward', out_shape=[pltpu.VMEM((OWN, D...  85.3 us

profile of v5, /device:TPU:2, one launch (start us, length us, event | category | flops | bytes accessed | tf_op | source)
XLA Modules:
  0.0 87.1 jit_solution(2933789646019244134)
XLA Ops:
  0.6 85.3 %ffn_backward.1 = (bf16[32,512]{1,0:T(8,128)(2,1)S(1)}, bf16[512,512]{1,0:T(8,128)(2,1)S(1)}, bf16[512,512]{1,0:T(8,128)(2,1)S(1)}, bf16[512,512]{1,0:T(8,128)(2,1)S(1)}) custom-call(bf16[32,512]{1,0:T(8,128)(2,1)} %x_in.1, bf16[32,512]{1,0:T(8,128)(2,1)} %cot_in.1, bf16[512,512]{1,0:T(8,128)(2,1)} %wg_in.1, bf16[512,512]{1,0:T(8,128)(2,1)} %wu_in.1, ...), custom_call_target="tpu_custom_call" | custom-call | tf_op jit(solution)/shard_map/ffn_backward/pallas_call | solution.py:400
  85.9 1.2 %publish.1 = (bf16[32,512]{1,0:T(8,128)(2,1)}, bf16[512,512]{1,0:T(8,128)(2,1)}, bf16[512,512]{1,0:T(8,128)(2,1)}, bf16[512,512]{1,0:T(8,128)(2,1)}) custom-call(bf16[32,512]{1,0:T(8,128)(2,1)S(1)} %get-tuple-element.8.refs_0_, bf16[512,512]{1,0:T(8,128)(2,1)S(1)} %get-tuple-element.9.refs_1_, bf16[512,512]{1,0:T(8,128)(2,1)S(1)} %get-tuple-element.10.refs_2_, ...), custom_call_target="tpu_custom_call" | custom-call | tf_op jit(solution)/shard_map/publish/pallas_call | solution.py:447
